TPU v7x, 256 devices: a whole 4x4x8 slice. The times are simulated.
256 devices in a mesh: grp: 8 (over x_hi, y), sp: 32 (over x_lo, z, core).
Axes of the slice: x: 4 (x_hi: 2, x_lo: 2; x = x_hi * 2 + x_lo), y: 4, z: 8, core: 2. Of those that a mesh axis runs over, the one named last changes fastest.
Arguments:
- queries: bfloat16 [32768, 8192], P(('grp', 'sp')), may hold values from -160 to 160
- keys: bfloat16 [32768, 1024], P(('grp', 'sp')), may hold values from -6 to 6
- values: bfloat16 [32768, 1024], P(('grp', 'sp')), may hold values from -6 to 6
Outputs:
- attended: bfloat16 [32768, 8192], P(('grp', 'sp'))
All inputs are finite; a program needn't handle non-finite values.
Results may differ from a plain program's by a relative error of at most 0.008.
Values may be sent and summed in bfloat16 or wider, within the bound.
A program may use at most 64 MiB of HBM per device.

v0:
```python
import jax
import jax.numpy as jnp
from jax import lax
from jax.sharding import PartitionSpec as P

QUERY_HEADS = 64
KEY_VALUE_HEADS = 8
HEAD_SIZE = 128
BLOCK_TOKENS = 1024


def from_root(value, axis, root):
    mine = lax.axis_index(axis) == root
    return lax.psum(jnp.where(mine, value, jnp.zeros_like(value)), axis)


def shards(queries, keys, values):
    tok_rows = queries.shape[0]
    shard_count = lax.axis_size("sp")
    heads_dev = QUERY_HEADS // shard_count
    grouped_query_rows = QUERY_HEADS // KEY_VALUE_HEADS
    group_span = tok_rows * shard_count
    score_scale = HEAD_SIZE ** (-0.5)
    query_split = queries.reshape(tok_rows, shard_count, heads_dev * HEAD_SIZE)
    query_heads = lax.all_to_all(query_split, "sp", split_axis=1, concat_axis=0, tiled=True)
    whole_keys, whole_values = (
        lax.all_gather(keys, "sp", axis=0, tiled=True),
        lax.all_gather(values, "sp", axis=0, tiled=True),
    )
    head_start = lax.axis_index("sp") * heads_dev // grouped_query_rows * HEAD_SIZE
    key_head = lax.dynamic_slice_in_dim(whole_keys, head_start, HEAD_SIZE, 1)
    value_head = lax.dynamic_slice_in_dim(whole_values, head_start, HEAD_SIZE, 1)
    anchor_k, anchor_v = (
        from_root(key_head[:BLOCK_TOKENS], "grp", 0),
        from_root(value_head[:BLOCK_TOKENS], "grp", 0),
    )
    context_block_count = group_span // BLOCK_TOKENS
    first_block = lax.axis_index("grp") * context_block_count
    blockwise_queries = query_heads.reshape(context_block_count, BLOCK_TOKENS, heads_dev, HEAD_SIZE)
    blockwise_keys = key_head.reshape(context_block_count, BLOCK_TOKENS, HEAD_SIZE)
    blockwise_values = value_head.reshape(context_block_count, BLOCK_TOKENS, HEAD_SIZE)
    positions = jnp.arange(BLOCK_TOKENS)
    causal = positions[:, None] >= positions[None, :]

    def attend_block(items):
        query_block, key_block, value_block, block_index = items
        local_scores = (
            jnp.einsum("qhd,kd->hqk", query_block, key_block, preferred_element_type=jnp.float32)
            * score_scale
        )
        local_scores = jnp.where(causal, local_scores, -1e30)
        anchor_scores = (
            jnp.einsum("qhd,kd->hqk", query_block, anchor_k, preferred_element_type=jnp.float32)
            * score_scale
        )
        anchor_scores = jnp.where(first_block + block_index > 0, anchor_scores, -1e30)
        local_max = jnp.max(local_scores, axis=-1)
        anchor_max = jnp.max(anchor_scores, axis=-1)
        top_score = jnp.maximum(local_max, anchor_max)
        local_weights = jnp.exp(local_scores - top_score[..., None])
        anchor_weights = jnp.exp(anchor_scores - top_score[..., None])
        total = jnp.sum(local_weights, axis=-1) + jnp.sum(anchor_weights, axis=-1)
        summed = jnp.einsum(
            "hqk,kd->qhd",
            local_weights.astype(jnp.bfloat16),
            value_block,
            preferred_element_type=jnp.float32,
        )
        summed = summed + jnp.einsum(
            "hqk,kd->qhd",
            anchor_weights.astype(jnp.bfloat16),
            anchor_v,
            preferred_element_type=jnp.float32,
        )
        result = summed / jnp.transpose(total)[..., None]
        return result.astype(jnp.bfloat16).reshape(BLOCK_TOKENS, heads_dev * HEAD_SIZE)

    outputs = lax.map(
        attend_block,
        (
            blockwise_queries,
            blockwise_keys,
            blockwise_values,
            jnp.arange(context_block_count, dtype=jnp.int32),
        ),
    )
    returned = lax.all_to_all(
        outputs.reshape(group_span, 1, heads_dev * HEAD_SIZE),
        "sp",
        split_axis=0,
        concat_axis=1,
        tiled=True,
    )
    return returned.reshape(tok_rows, QUERY_HEADS * HEAD_SIZE)


def solution(mesh):
    return jax.shard_map(
        shards,
        mesh=mesh,
        in_specs=(P(("grp", "sp"), None), P(("grp", "sp"), None), P(("grp", "sp"), None)),
        out_specs=P(("grp", "sp"), None),
        check_vma=False,
    )
```

profile of v0, /device:TPU:225, one launch (start us, length us, event | category | flops | bytes accessed | tf_op | source)
XLA Modules:
  0.0 439.7 jit_solution(12039372404460586013)
XLA Ops:
  8.0 3.2 copy.51
  11.2 7.2 %all-to-all-start = ((bf16[128,32,256]{2,0,1:T(8,128)(2,1)}), bf16[128,32,256]{2,0,1:T(8,128)(2,1)S(1)}, u32[]{:S(2)}, u32[]{:S(2)}) async-start(bf16[128,32,256]{2,0,1:T(8,128)(2,1)} %bitcast.119), calls=%async_computation | async-start | bytes 4194304 | tf_op jit(solution)/shard_map/all_to_all | solution.py:25
  18.6 67.2 %all-to-all-done = bf16[128,32,256]{2,0,1:T(8,128)(2,1)S(1)} async-done(((bf16[128,32,256]{2,0,1:T(8,128)(2,1)}), bf16[128,32,256]{2,0,1:T(8,128)(2,1)S(1)}, u32[]{:S(2)}, u32[]{:S(2)}) %all-to-all-start) | async-done | bytes 2097184 | tf_op jit(solution)/shard_map/all_to_all | solution.py:25
  89.7 27.5 %all-gather.3.cloned.1.call-done = bf16[4096,1024]{1,0:T(8,128)(2,1)} async-done(((bf16[128,1024]{1,0:T(8,128)(2,1)}), bf16[4096,1024]{1,0:T(8,128)(2,1)}) %all-gather.3.cloned.1.call-update) | async-done | bytes 8388624 | tf_op jit(solution)/shard_map/all_gather | solution.py:28
  119.0 71.3 %all-gather.5.cloned.1.call-done = bf16[4096,1024]{1,0:T(8,128)(2,1)} async-done(((bf16[128,1024]{1,0:T(8,128)(2,1)}), bf16[4096,1024]{1,0:T(8,128)(2,1)}) %all-gather.5.cloned.1.call-update) | async-done | bytes 8388624 | tf_op jit(solution)/shard_map/all_gather | solution.py:27
  196.7 82.4 %all-reduce.3.cloned.1.call-done = (bf16[1024,128]{1,0:T(8,128)(2,1)}, bf16[1024,128]{1,0:T(8,128)(2,1)}) async-done(((bf16[1024,128]{1,0:T(8,128)(2,1)}, bf16[1024,128]{1,0:T(8,128)(2,1)}), (bf16[1024,128]{1,0:T(8,128)(2,1)}, bf16[1024,128]{1,0:T(8,128)(2,1)})) %all-reduce.3.cloned.1.call-update) | async-done | bytes 524304 | tf_op jit(solution)/shard_map/psum | solution.py:14
  280.1 69.6 %while.11 = (s32[]{:T(128)}, bf16[4,1024,256]{2,1,0:T(8,128)(2,1)}, bf16[4,1024,128]{2,1,0:T(8,128)(2,1)}, bf16[4,1024,128]{2,1,0:T(8,128)(2,1)}, bf16[4,1024,2,...) while((s32[]{:T(128)}, bf16[4,1024,256]{2,1,0:T(8,128)(2,1)}, ...), condition=%wide.region_7.8_spmd.clone, body=%wide.region_2.7_spmd.clone.sunk | while | flops 2195451904 | bytes 62506640 | solution.py:78
  284.3 2.8 fusion.50
  287.2 3.6 fusion.52
  290.8 3.6 fusion.51
  301.7 2.8 fusion.50
  304.6 3.6 fusion.52
  308.2 3.6 fusion.51
  319.1 2.8 fusion.50
  322.0 3.6 fusion.52
  325.6 3.6 fusion.51
  336.5 2.8 fusion.50
  339.4 3.6 fusion.52
  343.0 3.6 fusion.51
  350.3 3.8 reduce
  356.1 60.8 %all_to_all.30 = bf16[32,2,16384]{2,1,0:T(2,128)(2,1)S(1)} all-to-all(bf16[32,2,16384]{2,1,0:T(2,128)(2,1)} %reshape.38), channel_id=1, replica_groups=mesh['grp'=8,'sp'=32] {'sp'}, dimensions={0} | all-to-all | bytes 4194304 | tf_op jit(solution)/shard_map/all_to_all | solution.py:87
  416.9 6.8 %reshape.39 = bf16[4096,1,256]{2,1,0:T(2,128)(2,1)} reshape(bf16[32,2,16384]{2,1,0:T(2,128)(2,1)S(1)} %all_to_all.30) | data formatting | bytes 4194304
  426.2 2.9 copy.33
  429.1 4.1 copy.34
  (55 shorter events, 46.3 us)
Async XLA Ops:
  6.5 110.7 %all-gather.3.cloned.1.call-start = ((), (), s32[]{:S(2)}) async-start(), calls=%async_computation.2 | async-start | bytes 8650752 | tf_op jit(solution)/shard_map/all_gather | solution.py:28
  7.3 183.0 %all-gather.5.cloned.1.call-start = ((), (), s32[]{:S(2)}) async-start(), calls=%async_computation.3 | async-start | bytes 8650752 | tf_op jit(solution)/shard_map/all_gather | solution.py:27
  11.2 74.6 %all-to-all-start = ((bf16[128,32,256]{2,0,1:T(8,128)(2,1)}), bf16[128,32,256]{2,0,1:T(8,128)(2,1)S(1)}, u32[]{:S(2)}, u32[]{:S(2)}) async-start(bf16[128,32,256]{2,0,1:T(8,128)(2,1)} %bitcast.119), calls=%async_computation | async-start | bytes 4194304 | tf_op jit(solution)/shard_map/all_to_all | solution.py:25
  18.5 260.6 %all-reduce.3.cloned.1.call-start = ((), (), s32[]{:S(2)}) async-start(), calls=%async_computation.4 | async-start | bytes 1048576 | tf_op jit(solution)/shard_map/psum | solution.py:14
  85.8 1.3 copy-start
Sparse Core Ops, SparseCore 0:
  9.2 107.9 all-gather.2
  119.1 71.1 all-gather.4
  193.0 86.0 all-reduce.2
where the time goes:
time: 447 us; the launch traced here: 440 us
  waiting for transfers between devices  250 us (56%)
  blocking collectives  60.8 us (14%)
  matrix products  42.8 us (10%)
  local copies, waits for them, and re-layouts  39.8 us (9%)
  other arithmetic  23.1 us (5%)
  between operations  13.2 us (3%)
  starting transfers between devices  7.33 us (2%)
    psum x1, waiting for transfers between devices, from_root(): return lax.psum(jnp.where(mine, value, jnp.zeros_like(value)), axis)  82.4 us
    all_gather x1, waiting for transfers between devices, shards(): lax.all_gather(keys, 'sp', axis=0, tiled=True)  71.3 us
    all_to_all x1, waiting for transfers between devices, shards(): lax.all_to_all(query_split, 'sp', split_axis=1, concat_axis=0, tiled=True)  67.2 us
    all_to_all x1, blocking collectives, shards(): lax.all_to_all(outputs.reshape(group_span, 1, heads_dev * HEAD_SIZE), 'sp...  60.8 us
    all_gather x1, waiting for transfers between devices, shards(): lax.all_gather(values, 'sp', axis=0, tiled=True)  27.5 us
    reduce_sum x4, other arithmetic, attend_block(): total = jnp.sum(local_weights, axis=-1) + jnp.sum(anchor_weights, axis=-1)  14.6 us
    dot_general x4, matrix products, attend_block(): jnp.einsum('hqk,kd->qhd', local_weights.astype(jnp.bfloat16), value_block...  14.4 us
    unnamed x6, local copies, waits for them, and re-layouts  13.8 us
  transfers between devices with their start and end apart: 4, of which 4 were waited for; matrix products, arithmetic and copies ran while one was open for 3% of the time, Pallas kernels for 0%

commit v1 on v0

v1 whole, which is shorter than its diff:
```python
import functools

import jax
import jax.numpy as jnp
from jax import lax
from jax.experimental import pallas as pl
from jax.experimental.pallas import tpu as pltpu
from jax.sharding import PartitionSpec as P

MESH = pl.DeviceIdType.MESH
HEAD = 128
HEADS = 4
GROUP = 8
TOKENS = 128
CHIP = 256
WIDE = HEADS * HEAD
SCALE = HEAD**-0.5 * 1.4426950408889634
LOW = -1e30
BF = jnp.bfloat16
F32 = jnp.float32
NT = (((1,), (1,)), ((), ()))
S_SCATTER, S_PLANES, S_FIRST, S_SECOND, S_UP, S_SKIP, S_ROUND, S_RELAY, S_PAIR, S_QUERY, S_OUT, S_COUNT = (
    0, 1, 2, 3, 7, 8, 9, 10, 11, 12, 13, 14)


def dev(x, y, z, c):
    return {"grp": (x // 2) * 4 + y, "sp": (x % 2) * 16 + z * 2 + c}


def kernel(q_hbm, k_hbm, v_hbm, o_hbm, qbuf, obuf, kloc, vloc, kanc, vanc, kfor, vfor, s0, s1, acc, tot, top,
           send, scat_sem, plane_sem, first_sem, second_sem, loc_sem, for_sem, query_sem, own_sem, out_sem, late):
    grp, sp = lax.axis_index("grp"), lax.axis_index("sp")
    x, y = (grp // 4) * 2 + sp // 16, grp % 4
    z, c = (sp // 2) % 8, sp % 2
    j = z % 4
    half = z - j
    low = z < 4
    other = 1 - c
    first_block = jnp.logical_and(x + y == 0, low)

    def remote(src, dst, ssem, rsem, where):
        pltpu.make_async_remote_copy(
            src_ref=src, dst_ref=dst, send_sem=ssem, recv_sem=rsem, device_id=where, device_id_type=MESH
        ).start()

    def wait_kib(sem, kib):
        ref = qbuf if kib == 2048 else kloc.at[pl.ds(0, kib)]
        pltpu.make_async_copy(ref, ref, sem).wait()

    def cols(h):
        return pl.ds(h * HEAD if isinstance(h, int) else pl.multiple_of(h * HEAD, HEAD), HEAD)

    def rows(start, count):
        return pl.ds(pl.multiple_of(start, 16), count)

    barrier = pltpu.get_barrier_semaphore()

    def greet(where):
        pl.semaphore_signal(barrier, 1, device_id=where, device_id_type=MESH)

    greet(dev(x, y, z, other))
    for d in range(1, 4):
        greet(dev((x + d) % 4, y, z, c))
        greet(dev(x, (y + d) % 4, z, c))
        for cc in range(2):
            greet(dev(x, y, half + (j + d) % 4, cc))

    @pl.when(low)
    def _():
        for cc in range(2):
            @pl.when(jnp.logical_or(x + y > 0, c != cc))
            def _():
                greet(dev(0, 0, z, cc))
            for d in range(4):
                greet(dev(x, y, 4 + d, cc))

    pl.semaphore_wait(barrier, 13 + jnp.where(low, jnp.where(first_block, 31, 0), 8))

    def own(ref, h, cc):
        return ref.at[:, pl.ds(cc * WIDE + h * HEAD, HEAD)]

    def send_own(h, zt, kdst, vdst, base, ssem, rsem):
        for cc in range(2):
            for src, dst in ((k_hbm, kdst), (v_hbm, vdst)):
                remote(own(src, h, cc), dst.at[rows(base + c * TOKENS, TOKENS), cols(h)], ssem, rsem, dev(x, y, zt, cc))

    mine = rows(j * CHIP + c * TOKENS, TOKENS)

    def half_of(ref, cc, width):
        return ref.at[:, pl.ds(pl.multiple_of(cc * width, width), width)]

    @pl.when(first_block)
    def _():
        for k in range(8):
            px, py = c * 2 + k // 4, k % 4
            for cc in range(2):
                for src, dst in ((k_hbm, kanc), (v_hbm, vanc)):
                    a = src.at[pl.ds(k * 16, 16), pl.ds(cc * WIDE, WIDE)]
                    b = dst.at[px, py, rows(z * 16, 16), :]
                    if k == 0 and cc == 0:
                        @pl.when(c == 0)
                        def _():
                            pltpu.make_async_copy(a, b, scat_sem).start()

                        @pl.when(c == 1)
                        def _():
                            remote(a, b, send.at[S_SCATTER], scat_sem, dev(px, py, z, cc))
                    else:
                        remote(a, b, send.at[S_SCATTER], scat_sem, dev(px, py, z, cc))

    @pl.when(j < 3)
    def _():
        for h in range(HEADS):
            send_own(h, z + 1, kloc, vloc, j * CHIP, send.at[S_UP], loc_sem.at[j * 4 + h])

    for src, dst in ((k_hbm, kloc), (v_hbm, vloc)):
        pltpu.make_async_copy(half_of(src, c, WIDE), dst.at[mine, :], own_sem).start()
        remote(half_of(src, other, WIDE), dst.at[mine, :], send.at[S_PAIR], own_sem, dev(x, y, z, other))
    for h in range(HEADS):
        wide = GROUP * HEAD
        to = qbuf.at[rows(c * TOKENS, TOKENS), pl.ds(h * wide, wide)]

        def part(cc):
            return q_hbm.at[:, pl.ds(pl.multiple_of(cc * (HEADS * wide) + h * wide, wide), wide)]

        pltpu.make_async_copy(part(c), to, query_sem.at[h]).start()
        remote(part(other), to, send.at[S_QUERY], query_sem.at[h], dev(x, y, z, other))

    @pl.when(jnp.logical_not(low))
    def _():
        def tell(zt, cc):
            pl.semaphore_signal(late, 1, device_id=dev(x, y, zt, cc), device_id_type=MESH)

        tell(7 - z, c)

        @pl.when(z == 7)
        def _():
            tell(1, c)

        @pl.when(z == 5)
        def _():
            tell(0, 0)
            tell(0, 1)

    @pl.when(low)
    def _():
        pl.semaphore_wait(late, jnp.where(z == 0, 3, jnp.where(z == 1, 2, 1)))

    @pl.when(j == 0)
    def _():
        for h in range(HEADS):
            send_own(h, (z + 5) % 8, kfor, vfor, 0, send.at[S_ROUND], for_sem.at[h])
        for h in range(HEADS):
            send_own(h, z + 2, kloc, vloc, 0, send.at[S_SKIP], loc_sem.at[h])

    wait_kib(scat_sem, 32)
    source = jnp.where(low, z, 7 - z)
    for ref in (kanc, vanc):
        piece = ref.at[x, y, rows(source * 16, 16), :]
        for d in range(1, 4):
            remote(piece, piece, send.at[S_PLANES], plane_sem, dev(x, y, half + (j + d) % 4, c))

        @pl.when(low)
        def _():
            remote(piece, piece, send.at[S_PLANES], scat_sem, dev(x, y, 7 - z, c))

    wait_kib(plane_sem, 96)

    for h in range(HEADS):
        for d in range(1, 4):
            a, b = kanc.at[x, y, :, cols(h)], vanc.at[x, y, :, cols(h)]
            remote(a, a, send.at[S_FIRST], first_sem.at[h], dev((x + d) % 4, y, z, c))
            remote(b, b, send.at[S_FIRST], first_sem.at[h], dev(x, (y + d) % 4, z, c))
    for h in range(HEADS):
        wait_kib(first_sem.at[h], 96)
        for d in range(1, 4):
            a, b = kanc.at[:, y, :, cols(h)], vanc.at[x, :, :, cols(h)]
            remote(a, a, send.at[S_SECOND + h], second_sem.at[h], dev(x, (y + d) % 4, z, c))
            remote(b, b, send.at[S_SECOND + h], second_sem.at[h], dev((x + d) % 4, y, z, c))

    def relay(h):
        def hand(kr, vr, krow, srow, zt, sem):
            for a, b in ((kr, kloc), (vr, vloc)):
                remote(
                    a.at[pl.ds(krow, CHIP), cols(h)], b.at[pl.ds(srow, CHIP), cols(h)], send.at[S_RELAY], sem, dev(x, y, zt, c)
                )

        @pl.when(j == 1)
        def _():
            wait_kib(for_sem.at[h], 128)
            hand(kfor, vfor, 0, 0, (z + 6) % 8, loc_sem.at[h])

        @pl.when(j == 2)
        def _():
            wait_kib(loc_sem.at[4 + h], 128)
            hand(kloc, vloc, CHIP, CHIP, z + 1, loc_sem.at[4 + h])

    relay(0)
    wait_kib(own_sem, 512)

    block_zero = jnp.where(first_block, 1e30, 0.0).astype(F32)
    own_rows = rows(j * CHIP, CHIP)

    def with_ones(v):
        return jnp.concatenate([v, jnp.ones_like(v)], axis=1)

    def qcols(h, g):
        return pl.ds(pl.multiple_of(h * (GROUP * HEAD) + g * HEAD, HEAD), HEAD)

    def dot_nt(a, b):
        return lax.dot_general(a, b, NT, preferred_element_type=F32)

    def staged(scores, finish):
        bufs = (s0, s1)
        scores(0, bufs[0])
        for g in range(GROUP):
            if g + 1 < GROUP:
                scores(g + 1, bufs[(g + 1) % 2])
            finish(g, bufs[g % 2])

    def anchor_and_own(h):
        def scores(g, buf):
            q = qbuf[:, qcols(h, g)]
            buf[:, :1024] = dot_nt(q, kanc[:, :, :, cols(h)].reshape(1024, HEAD))
            buf[:, 1024:] = dot_nt(q, kloc[own_rows, cols(h)])

        def finish(g, buf):
            sa, sd = buf[:, :1024], buf[:, 1024:]
            at = lax.broadcasted_iota(jnp.int32, (CHIP, CHIP), 0)
            key = lax.broadcasted_iota(jnp.int32, (CHIP, CHIP), 1)
            sd = jnp.where(at >= key, sd, LOW)
            m = jnp.maximum(jnp.max(sd, 1, keepdims=True), jnp.max(sa, 1, keepdims=True) - block_zero)
            pa = jnp.exp2((sa - (m + block_zero)) * SCALE).astype(BF)
            pd = jnp.exp2((sd - m) * SCALE).astype(BF)
            o = jnp.dot(pa, with_ones(vanc[:, :, :, cols(h)].reshape(1024, HEAD)), preferred_element_type=F32)
            o = o + jnp.dot(pd, with_ones(vloc[own_rows, cols(h)]), preferred_element_type=F32)
            at = qcols(h, g)
            acc[:, at] = o[:, :HEAD]
            tot[:, at] = o[:, HEAD:]
            top[:, at] = jnp.broadcast_to(m, (CHIP, HEAD))
            obuf[:, at] = (o[:, :HEAD] / o[:, HEAD:]).astype(BF)

        staged(scores, finish)

    def earlier(h, count):
        n = count * CHIP

        def scores(g, buf):
            buf[:, :n] = dot_nt(qbuf[:, qcols(h, g)], kloc[:n, cols(h)])

        def finish(g, buf):
            s = buf[:, :n]
            at = qcols(h, g)
            before = top[:, at]
            m = jnp.maximum(before, jnp.broadcast_to(jnp.max(s, 1, keepdims=True), (CHIP, HEAD)))
            p = jnp.exp2((s - jnp.concatenate([m] * (n // HEAD), axis=1)) * SCALE).astype(BF)
            o = jnp.dot(p, with_ones(vloc[:n, cols(h)]), preferred_element_type=F32)
            keep = jnp.exp2((before - m) * SCALE)
            obuf[:, at] = ((acc[:, at] * keep + o[:, :HEAD]) / (tot[:, at] * keep + o[:, HEAD:])).astype(BF)

        staged(scores, finish)

    def deliver(h):
        wide = GROUP * HEAD
        at = pl.ds(pl.multiple_of(h * wide, wide), wide)
        to = o_hbm.at[:, pl.ds(pl.multiple_of(c * (HEADS * wide) + h * wide, wide), wide)]
        remote(obuf.at[rows(other * TOKENS, TOKENS), at], to, send.at[S_OUT], out_sem, dev(x, y, z, other))
        pltpu.make_async_copy(obuf.at[rows(c * TOKENS, TOKENS), at], to, out_sem).start()

    def step(i, _):
        @pl.when(i < HEADS)
        def _():
            wait_kib(query_sem.at[i], 512)
            wait_kib(second_sem.at[i], 384)
            anchor_and_own(i)

            @pl.when(j == 0)
            def _():
                deliver(i)

        @pl.when(i < 2)
        def _():
            relay(i + 1)

        @pl.when(jnp.logical_and(i > 0, j > 0))
        def _():
            h = i - 1
            for count in range(1, 4):
                @pl.when(j == count)
                def _():
                    for slot in range(count):
                        if (count, slot) != (2, 1):
                            wait_kib(loc_sem.at[slot * 4 + h], 128)
                    earlier(h, count)
            deliver(h)

        @pl.when(i == 1)
        def _():
            relay(3)

        return 0

    lax.fori_loop(0, HEADS + 1, step, 0)

    wait_kib(out_sem, 2048)
    wait_kib(send.at[S_OUT], 1024)
    wait_kib(send.at[S_QUERY], 1024)
    wait_kib(send.at[S_PAIR], 256)
    wait_kib(send.at[S_FIRST], 384)
    for h in range(HEADS):
        wait_kib(send.at[S_SECOND + h], 384)

    @pl.when(low)
    def _():
        wait_kib(send.at[S_PLANES], 128)

    @pl.when(jnp.logical_not(low))
    def _():
        wait_kib(send.at[S_PLANES], 96)

    @pl.when(jnp.logical_and(first_block, c == 0))
    def _():
        wait_kib(send.at[S_SCATTER], 480)

    @pl.when(jnp.logical_and(first_block, c == 1))
    def _():
        wait_kib(send.at[S_SCATTER], 512)

    @pl.when(j < 3)
    def _():
        wait_kib(send.at[S_UP], 512)

    @pl.when(j == 0)
    def _():
        wait_kib(send.at[S_SKIP], 512)
        wait_kib(send.at[S_ROUND], 512)

    @pl.when(jnp.logical_or(j == 1, j == 2))
    def _():
        wait_kib(send.at[S_RELAY], 512)


def attend(queries, keys, values):
    dma = pltpu.SemaphoreType.DMA
    wide = HEADS * GROUP * HEAD
    return pl.pallas_call(
        kernel,
        out_shape=jax.ShapeDtypeStruct(queries.shape, BF),
        in_specs=[pl.BlockSpec(memory_space=pl.ANY)] * 3,
        out_specs=pl.BlockSpec(memory_space=pl.ANY),
        scratch_shapes=[
            pltpu.VMEM((CHIP, wide), BF),
            pltpu.VMEM((CHIP, wide), BF),
            pltpu.VMEM((1024, WIDE), BF),
            pltpu.VMEM((1024, WIDE), BF),
            pltpu.VMEM((4, 4, 64, WIDE), BF),
            pltpu.VMEM((4, 4, 64, WIDE), BF),
            pltpu.VMEM((CHIP, WIDE), BF),
            pltpu.VMEM((CHIP, WIDE), BF),
            pltpu.VMEM((CHIP, 1280), F32),
            pltpu.VMEM((CHIP, 1280), F32),
            pltpu.VMEM((CHIP, wide), F32),
            pltpu.VMEM((CHIP, wide), F32),
            pltpu.VMEM((CHIP, wide), F32),
            dma((S_COUNT,)),
            dma(()),
            dma(()),
            dma((4,)),
            dma((4,)),
            dma((12,)),
            dma((4,)),
            dma((4,)),
            dma(()),
            dma(()),
            pltpu.SemaphoreType.REGULAR,
        ],
        compiler_params=pltpu.CompilerParams(collective_id=0, has_side_effects=True, vmem_limit_bytes=56 << 20),
    )(queries, keys, values)


def solution(mesh):
    return jax.shard_map(
        attend,
        mesh=mesh,
        in_specs=(P(("grp", "sp"), None),) * 3,
        out_specs=P(("grp", "sp"), None),
        check_vma=False,
    )
```

time: 447 us -> 72.5 us (0.16); the launches traced: 440 us -> 72.3 us
  waiting for transfers between devices: 250 us -> 0 us
  Pallas kernels: 0 us -> 69.2 us
  blocking collectives: 60.8 us -> 0 us
  matrix products: 42.8 us -> 0 us
  local copies, waits for them, and re-layouts: 39.8 us -> 3.1 us
  other arithmetic: 23.1 us -> 0 us
  between operations: 13.2 us -> 0.01 us
  starting transfers between devices: 7.33 us -> 0 us
    all_gather x2 -> x0, waiting for transfers between devices: 98.8 us -> none  [the longest x1 71.3 us: shards(): lax.all_gather(keys, 'sp', axis=0, tiled=True)]
    psum x1 -> x0, waiting for transfers between devices: 82.4 us -> none  [from_root(): return lax.psum(jnp.where(mine, value, jnp.zeros_like(value)), axis)]
    pallas_call x0 -> x1, Pallas kernels: none -> 69.2 us  [attend(): pl.pallas_call(kernel, out_shape=jax.ShapeDtypeStruct(queries.shape, BF),...]
    all_to_all x1 -> x0, waiting for transfers between devices: 67.2 us -> none  [shards(): lax.all_to_all(query_split, 'sp', split_axis=1, concat_axis=0, tiled=True)]
    all_to_all x1 -> x0, blocking collectives: 60.8 us -> none  [shards(): lax.all_to_all(outputs.reshape(group_span, 1, heads_dev * HEAD_SIZE), 'sp...]
    dot_general x16 -> x0, matrix products: 42.8 us -> none  [the longest x4 14.4 us: attend_block(): jnp.einsum('hqk,kd->qhd', local_weights.astype(jnp.bfloat16), value_block...]
    reduce_sum x4 -> x0, other arithmetic: 14.6 us -> none  [attend_block(): total = jnp.sum(local_weights, axis=-1) + jnp.sum(anchor_weights, axis=-1)]
    unnamed x6 -> x1, local copies, waits for them, and re-layouts: 13.8 us -> 3.1 us
  transfers between devices with their start and end apart: 4 -> 0, of which waited for: 4 -> 0; matrix products, arithmetic and copies ran while one was open for 3% -> 0% of each run, Pallas kernels for 0% -> 0%
where the time goes in v1:
time: 72.5 us; the launch traced here: 72.3 us
  Pallas kernels  69.2 us (95%)
  local copies, waits for them, and re-layouts  3.1 us (4%)
    pallas_call x1, Pallas kernels, attend(): pl.pallas_call(kernel, out_shape=jax.ShapeDtypeStruct(queries.shape, BF),...  69.2 us
    unnamed x1, local copies, waits for them, and re-layouts  3.1 us

profile of v1, /device:TPU:225, one launch (start us, length us, event | category | flops | bytes accessed | tf_op | source)
XLA Modules:
  0.0 72.3 jit_solution(17139483850639193092)
XLA Ops:
  0.0 69.2 %shard_map.37 = bf16[128,8192]{1,0:T(8,128)(2,1)} custom-call(bf16[128,8192]{1,0:T(8,128)(2,1)} %q_hbm.1, bf16[128,1024]{1,0:T(8,128)(2,1)} %k_hbm.1, bf16[128,1024]{1,0:T(8,128)(2,1)} %v_hbm.1), custom_call_target="tpu_custom_call" | custom-call | tf_op jit(solution)/shard_map/pallas_call | solution.py:346
  69.3 3.1 %copy.5 = bf16[128,8192]{1,0:T(8,128)(2,1)} copy(bf16[128,8192]{1,0:T(8,128)(2,1)} %shard_map.37) | data formatting | bytes 4194304

commit v2 on v1

v2 whole, which is shorter than its diff:
```python
import functools

import jax
import jax.numpy as jnp
from jax import lax
from jax.experimental import pallas as pl
from jax.experimental.pallas import tpu as pltpu
from jax.sharding import PartitionSpec as P

MESH = pl.DeviceIdType.MESH
HEAD = 128
HEADS = 4
GROUP = 8
TOKENS = 128
CHIP = 256
WIDE = HEADS * HEAD
SCALE = HEAD**-0.5 * 1.4426950408889634
LOW = -1e30
ROUND_LOW, ROUND_HIGH = (2, 3), (0, 1, 2, 3)
PARTS = ((0, 2 * HEAD), (2 * HEAD, 2 * HEAD))
BF = jnp.bfloat16
F32 = jnp.float32
NT = (((1,), (1,)), ((), ()))
S_SCATTER, S_PLANES, S_FIRST, S_SECOND, S_UP, S_SKIP, S_ROUND, S_RELAY, S_PAIR, S_QUERY, S_OUT, S_COUNT = (
    0, 1, 2, 3, 7, 8, 9, 10, 11, 12, 13, 14)


def dev(x, y, z, c):
    return {"grp": (x // 2) * 4 + y, "sp": (x % 2) * 16 + z * 2 + c}


def kernel(q_hbm, k_hbm, v_hbm, o_hbm, qbuf, obuf, kloc, vloc, kanc, vanc, kfor, vfor, s0, s1, acc, tot, top,
           send, scat_sem, plane_sem, first_sem, second_sem, loc_sem, for_sem, query_sem, own_sem, out_sem, late):
    grp, sp = lax.axis_index("grp"), lax.axis_index("sp")
    x, y = (grp // 4) * 2 + sp // 16, grp % 4
    z, c = (sp // 2) % 8, sp % 2
    j = z % 4
    half = z - j
    low = z < 4
    other = 1 - c
    first_block = jnp.logical_and(x + y == 0, low)

    def remote(src, dst, ssem, rsem, where):
        pltpu.make_async_remote_copy(
            src_ref=src, dst_ref=dst, send_sem=send.at[ssem], recv_sem=rsem, device_id=where, device_id_type=MESH
        ).start()

    def wait_kib(sem, kib):
        ref = qbuf if kib == 2048 else kloc.at[pl.ds(0, kib)]
        pltpu.make_async_copy(ref, ref, sem).wait()

    def wait_sent(index, kib):
        wait_kib(send.at[index], kib)

    def cols(h):
        return pl.ds(h * HEAD if isinstance(h, int) else pl.multiple_of(h * HEAD, HEAD), HEAD)

    def rows(start, count):
        return pl.ds(pl.multiple_of(start, 16), count)

    barrier = pltpu.get_barrier_semaphore()

    def greet(where):
        pl.semaphore_signal(barrier, 1, device_id=where, device_id_type=MESH)

    greet(dev(x, y, z, other))
    for d in range(1, 4):
        greet(dev((x + d) % 4, y, z, c))
        greet(dev(x, (y + d) % 4, z, c))
        for cc in range(2):
            greet(dev(x, y, half + (j + d) % 4, cc))

    @pl.when(low)
    def _():
        for cc in range(2):
            @pl.when(jnp.logical_or(x + y > 0, c != cc))
            def _():
                greet(dev(0, 0, z, cc))
            for d in range(4):
                greet(dev(x, y, 4 + d, cc))

    pl.semaphore_wait(barrier, 13 + jnp.where(low, jnp.where(first_block, 31, 0), 8))

    @pl.when(jnp.logical_not(low))
    def _():
        def tell(zt, cc):
            pl.semaphore_signal(late, 1, device_id=dev(x, y, zt, cc), device_id_type=MESH)

        tell(7 - z, c)

        @pl.when(z == 7)
        def _():
            tell(1, c)

        @pl.when(z == 5)
        def _():
            tell(0, 0)
            tell(0, 1)

    @pl.when(first_block)
    def _():
        for part in range(2):
            for k in range(8):
                px, py = c * 2 + k // 4, k % 4
                for cc in range(2):
                    for src, dst in ((k_hbm, kanc), (v_hbm, vanc)):
                        lo, wide = PARTS[part]
                        a = src.at[pl.ds(k * 16, 16), pl.ds(cc * WIDE + lo, wide)]
                        b = dst.at[px, py, rows(z * 16, 16), pl.ds(lo, wide)]
                        if k == 0 and cc == 0:
                            @pl.when(c == 0)
                            def _():
                                pltpu.make_async_copy(a, b, scat_sem.at[part]).start()

                            @pl.when(c == 1)
                            def _():
                                remote(a, b, S_SCATTER, scat_sem.at[part], dev(px, py, z, cc))
                        else:
                            remote(a, b, S_SCATTER, scat_sem.at[part], dev(px, py, z, cc))

    def own(ref, h, cc):
        return ref.at[:, pl.ds(cc * WIDE + h * HEAD, HEAD)]

    def send_own(h, zt, kdst, vdst, base, ssem, rsem):
        for cc in range(2):
            for src, dst in ((k_hbm, kdst), (v_hbm, vdst)):
                remote(own(src, h, cc), dst.at[rows(base + c * TOKENS, TOKENS), cols(h)], ssem, rsem, dev(x, y, zt, cc))

    def up(heads):
        @pl.when(j < 3)
        def _():
            for h in heads:
                send_own(h, z + 1, kloc, vloc, j * CHIP, S_UP, loc_sem.at[j * 4 + h])

    def round_ring(heads):
        for h in heads:
            send_own(h, (z + 5) % 8, kfor, vfor, 0, S_ROUND, for_sem.at[h])

    mine = rows(j * CHIP + c * TOKENS, TOKENS)

    def half_of(ref, cc, width):
        return ref.at[:, pl.ds(pl.multiple_of(cc * width, width), width)]

    up((0, 1))
    for src, dst in ((k_hbm, kloc), (v_hbm, vloc)):
        pltpu.make_async_copy(half_of(src, c, WIDE), dst.at[mine, :], own_sem).start()
        remote(half_of(src, other, WIDE), dst.at[mine, :], S_PAIR, own_sem, dev(x, y, z, other))

    source = jnp.where(low, z, 7 - z)

    def pieces(part):
        lo, wide = PARTS[part]
        return [ref.at[x, y, rows(source * 16, 16), pl.ds(lo, wide)] for ref in (kanc, vanc)]

    def to_half(part):
        wait_kib(scat_sem.at[part], PARTS[part][1] // 16)
        for piece in pieces(part):
            for d in range(1, 4):
                remote(piece, piece, S_PLANES, plane_sem.at[part], dev(x, y, half + (j + d) % 4, c))

    def to_later(part):
        @pl.when(low)
        def _():
            for piece in pieces(part):
                remote(piece, piece, S_PLANES, scat_sem.at[part], dev(x, y, 7 - z, c))

    for h in range(HEADS):
        wide = GROUP * HEAD
        to = qbuf.at[rows(c * TOKENS, TOKENS), pl.ds(h * wide, wide)]

        def part_of(cc):
            return q_hbm.at[:, pl.ds(pl.multiple_of(cc * (HEADS * wide) + h * wide, wide), wide)]

        pltpu.make_async_copy(part_of(c), to, query_sem.at[h]).start()
        remote(part_of(other), to, S_QUERY, query_sem.at[h], dev(x, y, z, other))

    def hand(h, kr, vr, krow, srow, zt, sem):
        for a, b in ((kr, kloc), (vr, vloc)):
            remote(
                a.at[pl.ds(krow, CHIP), cols(h)], b.at[pl.ds(srow, CHIP), cols(h)], S_RELAY, sem, dev(x, y, zt, c)
            )

    def relay_next(h):
        wait_kib(loc_sem.at[4 + h], 128)
        hand(h, kloc, vloc, CHIP, CHIP, z + 1, loc_sem.at[4 + h])

    def relay(h):
        for at, heads in ((5, ROUND_LOW), (1, ROUND_HIGH)):
            if h in heads:
                @pl.when(z == at)
                def _():
                    wait_kib(for_sem.at[h], 128)
                    hand(h, kfor, vfor, 0, 0, (z + 6) % 8, loc_sem.at[h])

        for at, heads in ((2, ROUND_LOW), (6, ROUND_HIGH)):
            if h not in heads:
                @pl.when(z == at)
                def _():
                    wait_kib(loc_sem.at[h], 128)
                    hand(h, kloc, vloc, 0, 0, z + 1, loc_sem.at[h])

    block_zero = jnp.where(first_block, 1e30, 0.0).astype(F32)
    own_rows = rows(j * CHIP, CHIP)

    def with_ones(v):
        return jnp.concatenate([v, jnp.ones_like(v)], axis=1)

    def qcols(h, g):
        return pl.ds(pl.multiple_of(h * (GROUP * HEAD) + g * HEAD, HEAD), HEAD)

    def dot_nt(a, b):
        return lax.dot_general(a, b, NT, preferred_element_type=F32)

    def staged(scores, finish):
        bufs = (s0, s1)
        scores(0, bufs[0])
        for g in range(GROUP):
            if g + 1 < GROUP:
                scores(g + 1, bufs[(g + 1) % 2])
            finish(g, bufs[g % 2])

    def near(h, n):
        where = rows((j + 1) * CHIP - n, n)

        def scores(g, buf):
            buf[:, :n] = dot_nt(qbuf[:, qcols(h, g)], kloc[where, cols(h)])

        def finish(g, buf):
            at = lax.broadcasted_iota(jnp.int32, (CHIP, CHIP), 0)
            key = lax.broadcasted_iota(jnp.int32, (CHIP, CHIP), 1)
            s = jnp.where(at >= key, buf[:, n - CHIP : n], LOW)
            if n > CHIP:
                s = jnp.concatenate([buf[:, : n - CHIP], s], axis=1)
            weigh(h, g, s, vloc[where, cols(h)], 0.0, True, False)

        staged(scores, finish)

    def far(h, n):
        def scores(g, buf):
            buf[:, :n] = dot_nt(qbuf[:, qcols(h, g)], kloc[:n, cols(h)])

        def finish(g, buf):
            weigh(h, g, buf[:, :n], vloc[:n, cols(h)], 0.0, False, True)

        staged(scores, finish)

    def anchor(h, last):
        n = 1024

        def scores(g, buf):
            buf[...] = dot_nt(qbuf[:, qcols(h, g)], kanc[:, :, :, cols(h)].reshape(n, HEAD))

        def finish(g, buf):
            weigh(h, g, buf[...], vanc[:, :, :, cols(h)].reshape(n, HEAD), block_zero, False, last)

        staged(scores, finish)

    def weigh(h, g, s, v, away, first, last):
        at = qcols(h, g)
        m = jnp.broadcast_to(jnp.max(s, 1, keepdims=True), (CHIP, HEAD)) - away
        if not first:
            before = top[:, at]
            m = jnp.maximum(before, m)
        p = jnp.exp2((s - jnp.concatenate([m + away] * (s.shape[1] // HEAD), axis=1)) * SCALE).astype(BF)
        o = jnp.dot(p, with_ones(v), preferred_element_type=F32)
        weighted, total = o[:, :HEAD], o[:, HEAD:]
        if not first:
            keep = jnp.exp2((before - m) * SCALE)
            weighted, total = acc[:, at] * keep + weighted, tot[:, at] * keep + total
        if last:
            obuf[:, at] = (weighted / total).astype(BF)
        else:
            acc[:, at] = weighted
            tot[:, at] = total
            top[:, at] = m

    def early(h):
        wait_kib(query_sem.at[h], 512)

        @pl.when(j == 0)
        def _():
            near(h, CHIP)

        @pl.when(j > 0)
        def _():
            @pl.when(j != 2)
            def _():
                wait_kib(loc_sem.at[(j - 1) * 4 + h], 128)

            @pl.when(j == 2)
            def _():
                relay_next(h)

            near(h, 2 * CHIP)

    def late_part(h):
        @pl.when(j == 2)
        def _():
            handed = functools.reduce(
                jnp.logical_or,
                [
                    jnp.logical_and(z == at, h == hh)
                    for at, heads in ((2, ROUND_LOW), (6, ROUND_HIGH))
                    for hh in range(HEADS)
                    if hh not in heads
                ],
                False,
            )

            @pl.when(jnp.logical_not(handed))
            def _():
                wait_kib(loc_sem.at[h], 128)

            far(h, CHIP)

        @pl.when(j == 3)
        def _():
            wait_kib(loc_sem.at[h], 128)
            wait_kib(loc_sem.at[4 + h], 128)
            far(h, 2 * CHIP)

    def deliver(h):
        wide = GROUP * HEAD
        at = pl.ds(pl.multiple_of(h * wide, wide), wide)
        to = o_hbm.at[:, pl.ds(pl.multiple_of(c * (HEADS * wide) + h * wide, wide), wide)]
        remote(obuf.at[rows(other * TOKENS, TOKENS), at], to, S_OUT, out_sem, dev(x, y, z, other))
        pltpu.make_async_copy(obuf.at[rows(c * TOKENS, TOKENS), at], to, out_sem).start()

    def first(h):
        for d in range(1, 4):
            a, b = kanc.at[x, y, :, cols(h)], vanc.at[x, y, :, cols(h)]
            remote(a, a, S_FIRST, first_sem.at[h], dev((x + d) % 4, y, z, c))
            remote(b, b, S_FIRST, first_sem.at[h], dev(x, (y + d) % 4, z, c))

    def second(h):
        wait_kib(first_sem.at[h], 96)
        for d in range(1, 4):
            a, b = kanc.at[:, y, :, cols(h)], vanc.at[x, :, :, cols(h)]
            remote(a, a, S_SECOND + h, second_sem.at[h], dev(x, (y + d) % 4, z, c))
            remote(b, b, S_SECOND + h, second_sem.at[h], dev((x + d) % 4, y, z, c))

    wait_kib(own_sem, 512)
    pl.when(jnp.logical_not(low))(lambda: early(0))
    to_half(0)

    @pl.when(low)
    def _():
        pl.semaphore_wait(late, jnp.where(z == 0, 3, jnp.where(z == 1, 2, 1)))

    to_later(0)
    wait_kib(plane_sem.at[0], 48)
    first(0)
    first(1)
    to_half(1)
    pl.when(z == 4)(lambda: round_ring(ROUND_HIGH))
    to_later(1)
    up((2, 3))

    @pl.when(j == 0)
    def _():
        for h in range(HEADS):
            send_own(h, z + 2, kloc, vloc, 0, S_SKIP, loc_sem.at[h])

    pl.when(low)(lambda: early(0))
    second(0)
    second(1)
    early(1)
    wait_kib(plane_sem.at[1], 48)
    first(2)
    first(3)
    pl.when(z == 0)(lambda: round_ring(ROUND_LOW))
    relay(0)
    second(2)
    second(3)
    early(2)
    early(3)
    relay(1)
    relay(2)

    def step(h, _):
        wait_kib(second_sem.at[h], 384)

        @pl.when(j < 2)
        def _():
            anchor(h, True)

        @pl.when(j > 1)
        def _():
            anchor(h, False)

        @pl.when(h == 0)
        def _():
            relay(3)

        late_part(h)
        deliver(h)
        return 0

    lax.fori_loop(0, HEADS, step, 0)

    wait_kib(out_sem, 2048)
    wait_sent(S_OUT, 1024)
    wait_sent(S_QUERY, 1024)
    wait_sent(S_PAIR, 256)
    wait_sent(S_FIRST, 384)
    for h in range(HEADS):
        wait_sent(S_SECOND + h, 384)

    @pl.when(low)
    def _():
        wait_sent(S_PLANES, 128)

    @pl.when(jnp.logical_not(low))
    def _():
        wait_sent(S_PLANES, 96)

    @pl.when(jnp.logical_and(first_block, c == 0))
    def _():
        wait_sent(S_SCATTER, 480)

    @pl.when(jnp.logical_and(first_block, c == 1))
    def _():
        wait_sent(S_SCATTER, 512)

    @pl.when(j < 3)
    def _():
        wait_sent(S_UP, 512)

    @pl.when(j == 0)
    def _():
        wait_sent(S_SKIP, 512)

    for base, near, far in ((0, ROUND_LOW, ROUND_HIGH), (4, ROUND_HIGH, ROUND_LOW)):
        for at, index, count in (
            (0, S_ROUND, len(near)),
            (1, S_RELAY, len(far)),
            (2, S_RELAY, 2 * HEADS - len(near)),
        ):
            if count:
                @pl.when(z == base + at)
                def _():
                    wait_sent(index, 128 * count)


def place(src, dst, buf, sems):
    reads = [pltpu.make_async_copy(src.at[pl.ds(16 * i, 16)], buf.at[pl.ds(16 * i, 16)], sems.at[i]) for i in range(8)]
    writes = [pltpu.make_async_copy(buf.at[pl.ds(16 * i, 16)], dst.at[pl.ds(16 * i, 16)], sems.at[8 + i]) for i in range(8)]
    for copy in reads:
        copy.start()
    for read, write in zip(reads, writes):
        read.wait()
        write.start()
    for copy in writes:
        copy.wait()


def attend(queries, keys, values):
    dma = pltpu.SemaphoreType.DMA
    wide = HEADS * GROUP * HEAD
    result = pl.pallas_call(
        kernel,
        out_shape=jax.ShapeDtypeStruct(queries.shape, BF),
        in_specs=[pl.BlockSpec(memory_space=pl.ANY)] * 3,
        out_specs=pl.BlockSpec(memory_space=pl.ANY),
        scratch_shapes=[
            pltpu.VMEM((CHIP, wide), BF),
            pltpu.VMEM((CHIP, wide), BF),
            pltpu.VMEM((1024, WIDE), BF),
            pltpu.VMEM((1024, WIDE), BF),
            pltpu.VMEM((4, 4, 64, WIDE), BF),
            pltpu.VMEM((4, 4, 64, WIDE), BF),
            pltpu.VMEM((CHIP, WIDE), BF),
            pltpu.VMEM((CHIP, WIDE), BF),
            pltpu.VMEM((CHIP, 1024), F32),
            pltpu.VMEM((CHIP, 1024), F32),
            pltpu.VMEM((CHIP, wide), F32),
            pltpu.VMEM((CHIP, wide), F32),
            pltpu.VMEM((CHIP, wide), F32),
            dma((S_COUNT,)),
            dma((2,)),
            dma((2,)),
            dma((4,)),
            dma((4,)),
            dma((12,)),
            dma((4,)),
            dma((4,)),
            dma(()),
            dma(()),
            pltpu.SemaphoreType.REGULAR,
        ],
        compiler_params=pltpu.CompilerParams(collective_id=0, has_side_effects=True, vmem_limit_bytes=56 << 20),
    )(queries, keys, values)
    return pl.pallas_call(
        place,
        out_shape=jax.ShapeDtypeStruct(queries.shape, BF),
        in_specs=[pl.BlockSpec(memory_space=pl.ANY)],
        out_specs=pl.BlockSpec(memory_space=pl.ANY),
        scratch_shapes=[pltpu.VMEM((128, 8192), BF), pltpu.SemaphoreType.DMA((16,))],
    )(result)


def solution(mesh):
    return jax.shard_map(
        attend,
        mesh=mesh,
        in_specs=(P(("grp", "sp"), None),) * 3,
        out_specs=P(("grp", "sp"), None),
        check_vma=False,
    )
```

time: 72.5 us -> 58.3 us (0.80)
  Pallas kernels: 69.2 us -> 57.3 us
  local copies, waits for them, and re-layouts: 3.1 us -> 0 us
    pallas_call x1, Pallas kernels: 69.2 us -> 55 us  [attend(): pl.pallas_call(kernel, out_shape=jax.ShapeDtypeStruct(queries.shape, BF),...]
    unnamed x1 -> x0, local copies, waits for them, and re-layouts: 3.1 us -> none
    pallas_call x0 -> x1, Pallas kernels: none -> 2.4 us  [attend(): pl.pallas_call(place, out_shape=jax.ShapeDtypeStruct(queries.shape, BF),...]
where the time goes in v2:
time: 58.3 us; the launch traced here: 57.5 us
  Pallas kernels  57.3 us (98%)
    pallas_call x1, Pallas kernels, attend(): pl.pallas_call(kernel, out_shape=jax.ShapeDtypeStruct(queries.shape, BF),...  55 us
    pallas_call x1, Pallas kernels, attend(): pl.pallas_call(place, out_shape=jax.ShapeDtypeStruct(queries.shape, BF),...  2.4 us

profile of v2, /device:TPU:225, one launch (start us, length us, event | category | flops | bytes accessed | tf_op | source)
XLA Modules:
  0.0 57.5 jit_solution(5964283046941486133)
XLA Ops:
  0.0 55.0 %shard_map.37.src = bf16[128,8192]{1,0:T(8,128)(2,1)} custom-call(bf16[128,8192]{1,0:T(8,128)(2,1)} %q_hbm.1, bf16[128,1024]{1,0:T(8,128)(2,1)} %k_hbm.1, bf16[128,1024]{1,0:T(8,128)(2,1)} %v_hbm.1), custom_call_target="tpu_custom_call" | custom-call | tf_op jit(solution)/shard_map/pallas_call | solution.py:460
  55.0 2.4 %shard_map.38 = bf16[128,8192]{1,0:T(8,128)(2,1)} custom-call(bf16[128,8192]{1,0:T(8,128)(2,1)} %shard_map.37.src), custom_call_target="tpu_custom_call" | custom-call | tf_op jit(solution)/shard_map/pallas_call | solution.py:493

commit v3 on v2

--- a/solution.py
+++ b/solution.py
@@ -319,6 +319,17 @@
             wait_kib(loc_sem.at[4 + h], 128)
             far(h, 2 * CHIP)
 
+    def anchor_part(h):
+        wait_kib(second_sem.at[h], 384)
+
+        @pl.when(j < 2)
+        def _():
+            anchor(h, True)
+
+        @pl.when(j > 1)
+        def _():
+            anchor(h, False)
+
     def deliver(h):
         wide = GROUP * HEAD
         at = pl.ds(pl.multiple_of(h * wide, wide), wide)
@@ -370,23 +381,16 @@
     first(3)
     pl.when(z == 0)(lambda: round_ring(ROUND_LOW))
     relay(0)
+    anchor_part(0)
     second(2)
+    early(2)
     second(3)
-    early(2)
+    relay(1)
     early(3)
-    relay(1)
     relay(2)
 
     def step(h, _):
-        wait_kib(second_sem.at[h], 384)
-
-        @pl.when(j < 2)
-        def _():
-            anchor(h, True)
-
-        @pl.when(j > 1)
-        def _():
-            anchor(h, False)
+        pl.when(h > 0)(lambda: anchor_part(h))
 
         @pl.when(h == 0)
         def _():

time: 58.3 us -> 55.4 us (0.950)
  Pallas kernels: 57.3 us -> 55 us
    pallas_call x1, Pallas kernels: 55 us -> 52.6 us  [attend(): pl.pallas_call(kernel, out_shape=jax.ShapeDtypeStruct(queries.shape, BF),...]
where the time goes in v3:
time: 55.4 us; the launch traced here: 55.2 us
  Pallas kernels  55 us (99%)
    pallas_call x1, Pallas kernels, attend(): pl.pallas_call(kernel, out_shape=jax.ShapeDtypeStruct(queries.shape, BF),...  52.6 us
    pallas_call x1, Pallas kernels, attend(): pl.pallas_call(place, out_shape=jax.ShapeDtypeStruct(queries.shape, BF),...  2.4 us

profile of v3, /device:TPU:225, one launch (start us, length us, event | category | flops | bytes accessed | tf_op | source)
XLA Modules:
  0.0 55.2 jit_solution(7859514133508414473)
XLA Ops:
  0.0 52.6 %shard_map.37.src = bf16[128,8192]{1,0:T(8,128)(2,1)} custom-call(bf16[128,8192]{1,0:T(8,128)(2,1)} %q_hbm.1, bf16[128,1024]{1,0:T(8,128)(2,1)} %k_hbm.1, bf16[128,1024]{1,0:T(8,128)(2,1)} %v_hbm.1), custom_call_target="tpu_custom_call" | custom-call | tf_op jit(solution)/shard_map/pallas_call | solution.py:464
  52.6 2.4 %shard_map.38 = bf16[128,8192]{1,0:T(8,128)(2,1)} custom-call(bf16[128,8192]{1,0:T(8,128)(2,1)} %shard_map.37.src), custom_call_target="tpu_custom_call" | custom-call | tf_op jit(solution)/shard_map/pallas_call | solution.py:497
